TPU v7x, 32 devices: a whole 2x2x4 slice. The times are simulated.
32 devices in a mesh: groups: 2 (over x), wide: 16 (over z, y, core).
Axes of the slice: x: 2, y: 2, z: 4, core: 2. Of those that a mesh axis runs over, the one named last changes fastest.
Arguments:
- acts: bfloat16 [2, 512, 8192], P(None, 'groups', 'wide'), parts along dimension 1, may hold values from -6 to 6
- output_weight: bfloat16 [8192, 8192], P('wide'), may hold values from -0.0625 to 0.0625
- adapter_down_weight: bfloat16 [16, 8192, 64], P('wide'), may hold values from -0.0625 to 0.0625
- adapter_up_weight: bfloat16 [16, 64, 8192], P('wide'), may hold values from -0.75 to 0.75
- row_adapter_numbers: int32 [2, 512, 1], P(None, 'groups'), parts along dimension 1, may hold values from 0 to 15; in each aligned block of 256 rows (0 to 255, 256 to 511, ..., all dimensions but the last counted through in order) at most 48 rows name the same one
Outputs:
- projected: bfloat16 [2, 512, 8192], P(None, ('groups', 'wide')), parts along dimension 1
There are 2 independent parts, one for each index of `groups`. A program takes and returns all parts, laid end to end along the dimension named above; an argument that names none is the same for every part. Nothing has to cross between parts.
Inputs may be any that keep to these rules, and one draw needn't show every extreme that they name: `row_adapter_numbers`: in each step at most 48 rows name the same adapter, and in some step one adapter is named by exactly 48 rows.
All inputs are finite; a program needn't handle non-finite values.
Results may differ from a plain program's by a relative error of at most 0.0041.
Values may be sent and summed in bfloat16 or wider, within the bound.
A program may use at most 128 MiB of HBM per device.

v0:
```python
import jax
import jax.numpy as jnp
from jax import lax
from jax.sharding import PartitionSpec as P

CAP = 48


def slot_tables(row_adapter_numbers, pool_size):
    decode_step_count, decode_row_count = (
        row_adapter_numbers.shape[0],
        row_adapter_numbers.shape[1],
    )
    step_ids = row_adapter_numbers.reshape(decode_step_count, decode_row_count)
    onehot = (step_ids[:, :, None] == jnp.arange(pool_size, dtype=jnp.int32)[None, None, :]).astype(
        jnp.int32
    )
    before = jnp.cumsum(onehot, axis=1) - onehot
    within = jnp.sum(before * onehot, axis=2)
    slot_of_row = step_ids * CAP + within
    step_index = jnp.broadcast_to(
        jnp.arange(decode_step_count, dtype=jnp.int32)[:, None],
        (decode_step_count, decode_row_count),
    )
    row_numbers = jnp.broadcast_to(
        jnp.arange(decode_row_count, dtype=jnp.int32)[None, :],
        (decode_step_count, decode_row_count),
    )
    row_table = jnp.full((decode_step_count, pool_size * CAP), decode_row_count, jnp.int32)
    row_table = row_table.at[step_index, slot_of_row].set(row_numbers)
    return (slot_of_row, step_index, row_table)


def expand_held_rows(value_entries, adapter_up_weight, assigned_rows, decode_row_count):
    decode_step_count, held_row_count = (value_entries.shape[0], value_entries.shape[1])
    output_width = adapter_up_weight.shape[2]
    expanded_rows = jnp.einsum(
        "ihmx,hxz->ihmz", value_entries, adapter_up_weight, preferred_element_type=jnp.float32
    )
    expanded_rows = expanded_rows.reshape(decode_step_count, held_row_count * CAP, output_width)
    position_steps = jnp.broadcast_to(
        jnp.arange(decode_step_count, dtype=jnp.int32)[:, None],
        (decode_step_count, held_row_count * CAP),
    )
    adapter_delta = jnp.zeros((decode_step_count, decode_row_count, output_width), jnp.float32)
    return adapter_delta.at[position_steps, assigned_rows].add(expanded_rows, mode="drop")


def shards(acts, output_weight, adapter_down_weight, adapter_up_weight, row_adapter_numbers):
    devices = lax.axis_size("wide")
    owner_index = lax.axis_index("wide")
    decode_step_count, decode_row_count, feat_local = acts.shape
    held_row_count, adapter_rank_width, output_width = adapter_up_weight.shape
    pool_size = held_row_count * devices
    down_weight_local = lax.all_to_all(
        adapter_down_weight, "wide", split_axis=1, concat_axis=0, tiled=True
    )
    flat_rows = acts.reshape(decode_step_count * decode_row_count, feat_local)
    row_ids = row_adapter_numbers.reshape(decode_step_count * decode_row_count)
    selected = (row_ids[:, None] == jnp.arange(pool_size, dtype=jnp.int32)[None, :]).astype(
        jnp.float32
    )
    partial_value = jnp.einsum(
        "nf,afr->nar", flat_rows, down_weight_local, preferred_element_type=jnp.float32
    )
    shrunk = jnp.sum(partial_value * selected[:, :, None], axis=1)
    slot_of_row, step_index, row_table = slot_tables(row_adapter_numbers, pool_size)
    assigned_rows = lax.dynamic_slice_in_dim(
        row_table, owner_index * held_row_count * CAP, held_row_count * CAP, 1
    )
    low_rows = lax.psum(shrunk, "wide").astype(jnp.bfloat16)
    low_rows = low_rows.reshape(decode_step_count, decode_row_count, adapter_rank_width)
    padded = jnp.concatenate(
        [low_rows, jnp.zeros((decode_step_count, 1, adapter_rank_width), jnp.bfloat16)], axis=1
    )
    picked = jnp.take_along_axis(padded, assigned_rows[:, :, None], axis=1)
    value_entries = picked.reshape(decode_step_count, held_row_count, CAP, adapter_rank_width)
    adapter_delta = expand_held_rows(
        value_entries, adapter_up_weight, assigned_rows, decode_row_count
    )
    summed = (
        jnp.dot(flat_rows, output_weight, preferred_element_type=jnp.float32).reshape(
            decode_step_count, decode_row_count, output_width
        )
        + adapter_delta
    )
    return lax.psum_scatter(summed, "wide", scatter_dimension=1, tiled=True).astype(jnp.bfloat16)


def solution(mesh):
    in_specs = (
        P(None, "groups", "wide"),
        P("wide", None),
        P("wide", None, None),
        P("wide", None, None),
        P(None, "groups", None),
    )
    out_specs = P(None, ("groups", "wide"), None)
    return jax.shard_map(shards, mesh=mesh, in_specs=in_specs, out_specs=out_specs, check_vma=False)
```

profile of v0, /device:TPU:0, one launch (start us, length us, event | category | flops | bytes accessed | tf_op | source)
XLA Modules:
  0.0 423.0 jit_solution(2843052971515353789)
XLA Ops:
  6.5 9.3 %copy.10 = bf16[1,8192,64]{2,0,1:T(2,128)(2,1)} copy(bf16[1,8192,64]{1,2,0:T(8,128)(2,1)} %param.7) | data formatting | bytes 2097152 | tf_op args[2]
  15.8 0.5 broadcast.162
  16.3 45.2 %reduce.2 = bf16[8192,64]{1,0:T(8,128)(2,1)S(1)} reduce(bf16[8192,1,64]{2,1,0:T(2,128)(2,1)} %bitcast.62, bf16[]{:T(256)} %broadcast.162), dimensions={1}, to_apply=%bitcast.53.reduce_sub_computation | reduce | bytes 2097154
  61.5 0.0 copy-start.2
  61.5 2.3 reshape.123
  63.8 7.5 %all-to-all-start = ((bf16[16,2,16384]{2,1,0:T(2,128)(2,1)}), bf16[16,2,16384]{2,1,0:T(2,128)(2,1)S(1)}, u32[]{:S(2)}, u32[]{:S(2)}) async-start(bf16[16,2,16384]{2,1,0:T(2,128)(2,1)} %reshape.123), calls=%async_computation | async-start | bytes 2097152 | tf_op jit(solution)/shard_map/all_to_all | solution.py:55
  71.3 0.0 reduce-scatter.2.cloned.1.call-start
  71.4 1.2 reduce-window.6
  72.6 0.2 slice_reduce_fusion
  72.9 0.1 fusion.6
  73.0 24.2 %scatter_fusion = s32[2,768]{1,0:T(2,128)S(1)} fusion(s32[2,768]{1,0:T(2,128)S(1)} %broadcast_in_dim.17, s32[512]{0:T(512)S(1)} %bitcast.61, s32[512]{0:T(512)S(1)} %bitcast.72), kind=kCustom, calls=%fused_computation.1 | custom fusion | bytes 10240 | tf_op jit(solution)/shard_map/scatter | solution.py:30
  97.2 0.1 fusion.15
  97.3 0.1 reshape.94
  97.4 0.1 reshape.106
  97.5 0.1 compare_and_fusion
  97.6 11.6 %fusion = f32[2,256,8192]{2,1,0:T(8,128)} fusion(bf16[2,256,512]{2,1,0:T(8,128)(2,1)S(1)} %copy-done.1, bf16[512,8192]{1,0:T(8,128)(2,1)} %param.6), kind=kOutput, calls=%fused_computation.3 | convolution fusion | flops 4294967296 | bytes 25690112 | tf_op jit(solution)/shard_map/dot_general | solution.py:82
  109.2 0.0 all-to-all-done
  109.2 7.0 %reshape.124 = bf16[8192,1,64]{2,1,0:T(2,128)(2,1)} reshape(bf16[16,2,16384]{2,1,0:T(2,128)(2,1)S(1)} %all-to-all-done) | data formatting | bytes 2097152
  116.2 2.5 copy.17
  118.7 1.6 copy.12
  120.3 2.1 fusion.19
  122.4 0.3 multiply_reduce_fusion
  122.7 62.9 %all-reduce.2 = bf16[512,64]{0,1:T(8,128)(2,1)S(1)} all-reduce(f32[512,64]{0,1:T(8,128)S(1)} %multiply_reduce_fusion), channel_id=1, replica_groups=mesh['groups'=2,'wide'=16] {'wide'}, use_global_device_ids=true, to_apply=%region_5.6 | all-reduce | flops 32768 | bytes 196608 | tf_op jit(solution)/shard_map/psum | solution.py:71
  185.6 0.1 copy.13
  185.8 0.1 concatenate.11
  185.9 1.4 gather_fusion
  187.3 0.0 copy-done
  187.3 2.3 fusion.2
  189.6 44.7 %scatter_fusion.1 = f32[2,256,8192]{2,1,0:T(8,128)} fusion(f32[2,256,8192]{2,1,0:T(8,128)} %fusion, s32[96]{0:T(128)S(1)} %reshape.106, f32[96,8192]{1,0:T(8,128)} %bitcast.65), kind=kCustom, calls=%fused_computation.2 | custom fusion | flops 786432 | bytes 9437952 | tf_op jit(solution)/shard_map/scatter-add | solution.py:46
  234.3 0.0 reduce-scatter.2.cloned.1.call-update
  234.4 179.7 %reduce-scatter.2.cloned.1.call-done = f32[2,16,8192]{2,1,0:T(8,128)} async-done(((f32[2,256,8192]{2,1,0:T(8,128)}), f32[2,16,8192]{2,1,0:T(8,128)}) %reduce-scatter.2.cloned.1.call-update) | async-done | bytes 1048592 | tf_op jit(solution)/shard_map/reduce_scatter | solution.py:87
  414.1 2.1 convert_element_type.24
  (14 shorter events, 0.1 us)
Async XLA Ops:
  6.5 180.8 %copy-start = (bf16[1,64,8192]{2,1,0:T(8,128)(2,1)S(1)}, bf16[1,64,8192]{2,1,0:T(8,128)(2,1)}, u32[]{:S(2)}) copy-start(bf16[1,64,8192]{2,1,0:T(8,128)(2,1)} %param.8) | copy-start | bytes 3145732
  61.5 9.9 %copy-start.2 = (s32[2,256,1]{1,2,0:T(1,128)S(1)}, s32[2,256,1]{1,2,0:T(1,128)}, u32[]{:S(2)}) copy-start(s32[2,256,1]{1,2,0:T(1,128)} %param.9) | copy-start | bytes 6148
  63.8 33.8 %copy-start.1 = (bf16[2,256,512]{2,1,0:T(8,128)(2,1)S(1)}, bf16[2,256,512]{2,1,0:T(8,128)(2,1)}, u32[]{:S(2)}) copy-start(bf16[2,256,512]{2,1,0:T(8,128)(2,1)} %param.5) | copy-start | bytes 1572868
  63.8 45.4 %all-to-all-start = ((bf16[16,2,16384]{2,1,0:T(2,128)(2,1)}), bf16[16,2,16384]{2,1,0:T(2,128)(2,1)S(1)}, u32[]{:S(2)}, u32[]{:S(2)}) async-start(bf16[16,2,16384]{2,1,0:T(2,128)(2,1)} %reshape.123), calls=%async_computation | async-start | bytes 2097152 | tf_op jit(solution)/shard_map/all_to_all | solution.py:55
  71.3 342.7 %reduce-scatter.2.cloned.1.call-start = ((), (), s32[]{:S(2)}) async-start(), calls=%async_computation.2 | async-start | bytes 17825792 | tf_op jit(solution)/shard_map/reduce_scatter | solution.py:87
Sparse Core Ops, SparseCore 0:
  234.5 179.5 reduce-scatter.1
where the time goes:
time: 424 us; the launch traced here: 423 us
  waiting for transfers between devices  180 us (42%)
  other arithmetic  93.8 us (22%)
  blocking collectives  62.9 us (15%)
  local copies, waits for them, and re-layouts  49.5 us (12%)
  matrix products  16 us (4%)
  between operations  13.6 us (3%)
  starting transfers between devices  7.56 us (2%)
    reduce_scatter x1, waiting for transfers between devices, shards(): lax.psum_scatter(summed, 'wide', scatter_dimension=1, tiled=True)  180 us
    psum x1, blocking collectives, shards(): low_rows = lax.psum(shrunk, 'wide').astype(jnp.bfloat16)  62.9 us
    unnamed x1, other arithmetic  45.2 us
    scatter-add x1, other arithmetic, expand_held_rows(): adapter_delta.at[position_steps, assigned_rows]  44.7 us
    scatter x1, local copies, waits for them, and re-layouts, slot_tables(): row_table = row_table.at[step_index, slot_of_row].set(row_numbers)  24.2 us
    unnamed x14, local copies, waits for them, and re-layouts  21.5 us
    dot_general x1, matrix products, shards(): jnp.dot(flat_rows, output_weight, preferred_element_type=jnp.float32)  11.6 us
  transfers between devices with their start and end apart: 2, of which 1 were waited for; matrix products, arithmetic and copies ran while one was open for 9% of the time, Pallas kernels for 0%

commit v1 on v0

v1 whole, which is shorter than its diff:
```python
import functools

import jax
import jax.numpy as jnp
from jax import lax
from jax.experimental import pallas as pl
from jax.experimental.pallas import tpu as pltpu
from jax.sharding import PartitionSpec as P

CHUNKS = 8


def kernel(
    devices,
    stages,
    ids_ref,
    acts_ref,
    weight_ref,
    down_ref,
    up_ref,
    out_ref,
    acts_sib,
    weight_own,
    weight_sib,
    down_all,
    up_pair,
    total,
    low_part,
    low_got,
    low_all,
    low_mine,
    swap,
    *rest,
):
    sends, gots = rest[:stages], rest[stages : 2 * stages]
    (
        acts_sem,
        up_sem,
        weight_send,
        weight_recv,
        weight_local,
        down_send,
        down_recv,
        low_send,
        low_recv,
        all_send,
        all_recv,
        half_send,
        half_recv,
        swap_send,
        swap_recv,
    ) = rest[2 * stages :]
    me = lax.axis_index("wide")
    core = lax.rem(me, 2)
    chip = me // 2
    sibling = me + 1 - 2 * core
    rows, feats = acts_ref.shape
    rank = up_ref.shape[0]
    chunks, _, width = weight_own.shape
    half_columns = chunks * width
    block = rows // devices

    barrier = pltpu.get_barrier_semaphore()

    def greet(i, carry):
        pl.semaphore_signal(
            barrier,
            inc=1,
            device_id={"wide": lax.rem(me + i, devices)},
            device_id_type=pl.DeviceIdType.MESH,
        )
        return carry

    lax.fori_loop(1, devices, greet, 0)
    pl.semaphore_wait(barrier, devices - 1)

    def remote(src, dst, send, recv, to):
        return pltpu.make_async_remote_copy(
            src_ref=src,
            dst_ref=dst,
            send_sem=send,
            recv_sem=recv,
            device_id={"wide": to},
            device_id_type=pl.DeviceIdType.MESH,
        )

    def down_copy(to, owner):
        return remote(
            down_ref.at[to],
            down_all.at[pl.ds(pl.multiple_of(owner * rank, rank), rank)],
            down_send.at[to],
            down_recv.at[owner],
            to,
        )

    def low_copy(to, owner):
        return remote(
            low_part.at[to], low_got.at[owner], low_send.at[to], low_recv.at[owner], to
        )

    def all_copy(to, owner):
        return remote(
            low_all.at[owner], low_all.at[owner], all_send.at[to], all_recv.at[owner], to
        )

    def weight_copy(k):
        start = pl.multiple_of((1 - core) * half_columns + k * width, width)
        return remote(
            weight_ref.at[:, pl.ds(start, width)],
            weight_sib.at[k],
            weight_send.at[k],
            weight_recv.at[k],
            sibling,
        )

    def weight_fetch(k):
        start = pl.multiple_of(core * half_columns + k * width, width)
        return pltpu.make_async_copy(
            weight_ref.at[:, pl.ds(start, width)], weight_own.at[k], weight_local.at[k]
        )

    def each_peer(action):
        def one(i, carry):
            action(lax.rem(me + i, devices))
            return carry

        lax.fori_loop(1, devices, one, 0)

    def each_chunk(action):
        def one(k, carry):
            action(k)
            return carry

        lax.fori_loop(0, chunks, one, 0)

    own_rank = pl.ds(pl.multiple_of(core * rank, rank), rank)
    acts_copy = remote(acts_ref, acts_sib, acts_sem.at[0], acts_sem.at[1], sibling)
    up_copy = remote(
        up_ref.at[:, pl.ds(pl.multiple_of((1 - core) * half_columns, width), half_columns)],
        up_pair.at[own_rank],
        up_sem.at[0],
        up_sem.at[1],
        sibling,
    )
    up_fetch = pltpu.make_async_copy(
        up_ref.at[:, pl.ds(pl.multiple_of(core * half_columns, width), half_columns)],
        up_pair.at[own_rank],
        up_sem.at[2],
    )
    down_fetch = pltpu.make_async_copy(
        down_ref.at[me],
        down_all.at[pl.ds(pl.multiple_of(me * rank, rank), rank)],
        down_send.at[me],
    )
    each_peer(lambda peer: down_copy(peer, me).start())
    down_fetch.start()
    acts_copy.start()

    def load(k):
        weight_fetch(k).start()
        weight_copy(k).start()

    each_chunk(load)
    up_copy.start()
    up_fetch.start()

    acts_copy.wait_recv()

    def base(k):
        weight_fetch(k).wait()
        weight_copy(k).wait_recv()
        total[k] = jnp.dot(
            acts_ref[...], weight_own[k], preferred_element_type=jnp.float32
        ) + jnp.dot(acts_sib[...], weight_sib[k], preferred_element_type=jnp.float32)

    each_chunk(base)

    down_fetch.wait()
    each_peer(lambda peer: down_copy(me, peer).wait_recv())
    odd = (lax.broadcasted_iota(jnp.int32, (rows, 2 * rank), 1) >= rank).astype(jnp.int32)
    number = ids_ref[...] - odd
    low_part[...] = jnp.zeros_like(low_part)

    def shrink(j, carry):
        pair = down_all[pl.ds(pl.multiple_of(j * 2 * rank, 2 * rank), 2 * rank)]
        part = lax.dot_general(
            acts_ref[...], pair, (((1,), (1,)), ((), ())), preferred_element_type=jnp.float32
        )
        part = jnp.where(number == 2 * j, part, 0.0)
        low_part[...] += part.reshape(devices, block, 2 * rank)
        return carry

    lax.fori_loop(0, devices // 2, shrink, 0)
    each_peer(lambda peer: low_copy(peer, me).start())

    def gather(i, value):
        peer = lax.rem(me + i, devices)
        low_copy(me, peer).wait_recv()
        return value + low_got[peer]

    low_all[me] = lax.fori_loop(1, devices, gather, low_part[me]).astype(jnp.bfloat16)
    each_peer(lambda peer: all_copy(peer, me).start())
    each_peer(lambda peer: all_copy(me, peer).wait_recv())
    everything = low_all[...].astype(jnp.float32).reshape(rows, 2 * rank)
    low_mine[...] = jnp.where(number == 2 * chip, everything, 0.0).astype(jnp.bfloat16)
    up_fetch.wait()
    up_copy.wait_recv()

    bits = [lax.rem(chip // 2**s, 2) for s in range(stages)]
    partners = [me + 2 ** (s + 1) * (1 - 2 * bits[s]) for s in range(stages)]

    def half_copy(s, k):
        return remote(
            sends[s].at[k],
            gots[s].at[k],
            half_send.at[s * chunks + k],
            half_recv.at[s * chunks + k],
            partners[s],
        )

    half = rows // 2

    def delta(k, start):
        return jnp.dot(
            low_mine[pl.ds(start, half)],
            up_pair[:, pl.ds(pl.multiple_of(k * width, width), width)],
            preferred_element_type=jnp.float32,
        )

    away = pl.multiple_of((1 - bits[0]) * half, half)
    kept = pl.multiple_of(bits[0] * half, half)

    def first(k):
        sends[0][k] = (total[k, pl.ds(away, half)] + delta(k, away)).astype(jnp.bfloat16)
        half_copy(0, k).start()

    def second(k):
        total[k, pl.ds(kept, half)] += delta(k, kept)

    each_chunk(first)
    each_chunk(second)

    def swap_copy(k):
        return remote(
            swap.at[k],
            out_ref.at[core * chunks + k],
            swap_send.at[k],
            swap_recv.at[k],
            sibling,
        )

    def finish(s, k, offset, size):
        half_copy(s, k).wait_recv()
        small = size // 2
        last = s == stages - 1
        bit = core if last else bits[s + 1]
        there = pl.multiple_of((1 - bit) * small, small)
        here = pl.multiple_of(bit * small, small)
        away = total[k, pl.ds(pl.multiple_of(offset + there, small), small)] + gots[s][
            k, pl.ds(there, small)
        ].astype(jnp.float32)
        if last:
            swap[k] = away.astype(jnp.bfloat16)
            swap_copy(k).start()
        else:
            sends[s + 1][k] = away.astype(jnp.bfloat16)
            half_copy(s + 1, k).start()
        mine = pl.ds(pl.multiple_of(offset + here, small), small)
        value = total[k, mine] + gots[s][k, pl.ds(here, small)].astype(jnp.float32)
        if last:
            out_ref[core * chunks + k] = value.astype(jnp.bfloat16)
        else:
            total[k, mine] = value

    offsets, sizes = [kept], [half]
    for s in range(1, stages):
        sizes.append(sizes[-1] // 2)
        offsets.append(offsets[-1] + bits[s] * sizes[-1])

    def step(t, carry):
        for s in range(stages):

            @pl.when((t >= s) & (t - s < chunks))
            def _():
                finish(s, t - s, offsets[s], sizes[s])

        return carry

    lax.fori_loop(0, chunks + stages - 1, step, 0)

    other = 1 - core

    def close(k):
        remote(
            swap.at[k],
            out_ref.at[other * chunks + k],
            swap_send.at[k],
            swap_recv.at[k],
            sibling,
        ).wait_recv()
        swap_copy(k).wait_send()
        weight_copy(k).wait_send()
        for s in range(stages):
            half_copy(s, k).wait_send()

    each_chunk(close)

    def close_peer(peer):
        down_copy(peer, me).wait_send()
        low_copy(peer, me).wait_send()
        all_copy(peer, me).wait_send()

    each_peer(close_peer)
    acts_copy.wait_send()
    up_copy.wait_send()


def shards(devices, acts, weight, down, up, numbers):
    steps, rows, feats = acts.shape
    rank, columns = up.shape[1:]
    chips = devices // 2
    stages = chips.bit_length() - 1
    block = rows // devices
    total_rows = steps * rows
    width = columns // 2 // CHUNKS
    order = tuple(range(stages, 0, -1)) + (stages + 1, 0, stages + 2, stages + 3)

    def arranged(array):
        array = array.reshape((steps,) + (2,) * stages + (2, block, array.shape[-1]))
        return array.transpose(order).reshape(total_rows, array.shape[-1])

    down = down.reshape(devices, feats, rank).swapaxes(1, 2)
    bf16, f32 = jnp.bfloat16, jnp.float32
    low_block = (devices, total_rows // devices, 2 * rank)
    halves = [(CHUNKS, total_rows >> (s + 1), width) for s in range(stages)]
    dma = pltpu.SemaphoreType.DMA
    out = pl.pallas_call(
        functools.partial(kernel, devices, stages),
        out_shape=jax.ShapeDtypeStruct((2 * CHUNKS, steps * block, width), bf16),
        in_specs=[
            pl.BlockSpec(memory_space=pltpu.VMEM),
            pl.BlockSpec(memory_space=pltpu.VMEM),
            pl.BlockSpec(memory_space=pl.ANY),
            pl.BlockSpec(memory_space=pl.ANY),
            pl.BlockSpec(memory_space=pl.ANY),
        ],
        out_specs=pl.BlockSpec(memory_space=pltpu.VMEM),
        scratch_shapes=[
            pltpu.VMEM((total_rows, feats), bf16),
            pltpu.VMEM((CHUNKS, feats, width), bf16),
            pltpu.VMEM((CHUNKS, feats, width), bf16),
            pltpu.VMEM((devices * rank, feats), bf16),
            pltpu.VMEM((2 * rank, columns // 2), bf16),
            pltpu.VMEM((CHUNKS, total_rows, width), f32),
            pltpu.VMEM(low_block, f32),
            pltpu.VMEM(low_block, f32),
            pltpu.VMEM(low_block, bf16),
            pltpu.VMEM((total_rows, 2 * rank), bf16),
            pltpu.VMEM((CHUNKS, steps * block, width), bf16),
        ]
        + [pltpu.VMEM(shape, bf16) for shape in halves]
        + [pltpu.VMEM(shape, bf16) for shape in halves]
        + [dma((2,)), dma((3,))]
        + [dma((CHUNKS,))] * 3
        + [dma((devices,))] * 6
        + [dma((stages * CHUNKS,))] * 2
        + [dma((CHUNKS,))] * 2,
        compiler_params=pltpu.CompilerParams(
            collective_id=0, has_side_effects=True, vmem_limit_bytes=58 * 1024 * 1024
        ),
    )(arranged(numbers), arranged(acts), weight, down, up.reshape(rank, columns))
    out = out.reshape(2 * CHUNKS, steps, block, width).transpose(1, 2, 0, 3)
    return out.reshape(steps, block, columns)


def solution(mesh):
    in_specs = (
        P(None, "groups", "wide"),
        P("wide", None),
        P("wide", None, None),
        P("wide", None, None),
        P(None, "groups", None),
    )
    out_specs = P(None, ("groups", "wide"), None)
    return jax.shard_map(
        functools.partial(shards, mesh.shape["wide"]),
        mesh=mesh,
        in_specs=in_specs,
        out_specs=out_specs,
        check_vma=False,
    )
```

time: 424 us -> 117 us (0.28)
  waiting for transfers between devices: 180 us -> 0 us
  Pallas kernels: 0 us -> 108 us
  other arithmetic: 93.8 us -> 0.7 us
  blocking collectives: 62.9 us -> 0 us
  local copies, waits for them, and re-layouts: 49.5 us -> 7.88 us
  matrix products: 16 us -> 0 us
  between operations: 13.6 us -> 0.02 us
  starting transfers between devices: 7.56 us -> 0 us
    reduce_scatter x1 -> x0, waiting for transfers between devices: 180 us -> none  [shards(): lax.psum_scatter(summed, 'wide', scatter_dimension=1, tiled=True)]
    pallas_call x0 -> x1, Pallas kernels: none -> 108 us  [shards(): pl.pallas_call(functools.partial(kernel, devices, stages), out_shape=jax....]
    psum x1 -> x0, blocking collectives: 62.9 us -> none  [shards(): low_rows = lax.psum(shrunk, 'wide').astype(jnp.bfloat16)]
    scatter-add x1 -> x0, other arithmetic: 44.7 us -> none  [expand_held_rows(): adapter_delta.at[position_steps, assigned_rows]]
    unnamed x1, other arithmetic: 45.2 us -> 0.7 us
    scatter x1 -> x0, local copies, waits for them, and re-layouts: 24.2 us -> none  [slot_tables(): row_table = row_table.at[step_index, slot_of_row].set(row_numbers)]
    unnamed x14 -> x1, local copies, waits for them, and re-layouts: 21.5 us -> 1.58 us
    dot_general x2 -> x0, matrix products: 13.9 us -> none  [the longest x1 11.6 us: shards(): jnp.dot(flat_rows, output_weight, preferred_element_type=jnp.float32)]
  transfers between devices with their start and end apart: 2 -> 0, of which waited for: 1 -> 0; matrix products, arithmetic and copies ran while one was open for 9% -> 0% of each run, Pallas kernels for 0% -> 0%
where the time goes in v1:
time: 117 us
  Pallas kernels  108 us (92%)
  local copies, waits for them, and re-layouts  7.88 us (7%)
    pallas_call x1, Pallas kernels, shards(): pl.pallas_call(functools.partial(kernel, devices, stages), out_shape=jax....  108 us

profile of v1, /device:TPU:0, one launch (start us, length us, event | category | flops | bytes accessed | tf_op | source)
XLA Modules:
  0.0 116.7 jit_solution(4884191785375815181)
XLA Ops:
  0.0 1.6 %copy.15 = bf16[8,8,16,512]{3,2,1,0:T(8,128)(2,1)S(1)} copy(bf16[8,8,16,512]{3,1,2,0:T(8,128)(2,1)} %bitcast.28) | data formatting | bytes 2097152
  1.6 1.6 %copy.18 = bf16[16,512,64]{1,2,0:T(8,128)(2,1)} copy(bf16[16,512,64]{1,0,2:T(8,128)(2,1)S(1)} %bitcast.24) | data formatting | bytes 2097152 | tf_op jit(solution)/shard_map/reshape | solution.py:332
  3.1 1.9 %copy.10 = bf16[2,2,2,2,2,16,512]{6,5,0,4,1,2,3:T(8,128)(2,1)} copy(bf16[2,2,2,2,2,16,512]{6,5,4,3,2,1,0:T(8,128)(2,1)} %bitcast.29) | data formatting | bytes 1048576 | tf_op jit(solution)/shard_map/reshape | solution.py:329
  5.0 0.7 reduce
  5.7 0.1 reshape.24
  5.8 0.9 reshape.32.ids_ref
  6.7 108.1 %shard_map.55 = bf16[16,32,512]{2,1,0:T(8,128)(2,1)} custom-call(s32[512,1]{1,0:T(8,128)} %reshape.32.ids_ref, bf16[512,512]{1,0:T(8,128)(2,1)} %bitcast.25, bf16[512,8192]{1,0:T(8,128)(2,1)} %weight_ref.1, bf16[16,64,512]{2,1,0:T(8,128)(2,1)} %bitcast.23, bf16[64,8192]{1,0:T(8,128)(2,1)} %bitcast.27), custom_call_target="tpu_custom_call" | custom-call | tf_op jit(solution)/shard_map/pallas_call | solution.py:337
  114.9 1.9 %copy.14 = bf16[16,2,2,8,512]{4,3,0,2,1:T(8,128)(2,1)} copy(bf16[16,2,2,8,512]{4,3,2,1,0:T(8,128)(2,1)} %bitcast.26) | data formatting | bytes 1048576 | tf_op jit(solution)/shard_map/reshape | solution.py:373
  (1 shorter events, 0.0 us)

commit v2 on v1

--- a/solution.py
+++ b/solution.py
@@ -8,10 +8,12 @@
 from jax.sharding import PartitionSpec as P
 
 CHUNKS = 8
+EARLY = 3
 
 
 def kernel(
     devices,
+    groups,
     stages,
     ids_ref,
     acts_ref,
@@ -24,11 +26,14 @@
     weight_sib,
     down_all,
     up_pair,
+    up_far,
     total,
+    low_sum,
     low_part,
     low_got,
     low_all,
     low_mine,
+    low_far,
     swap,
     *rest,
 ):
@@ -36,11 +41,13 @@
     (
         acts_sem,
         up_sem,
+        far_sem,
         weight_send,
         weight_recv,
         weight_local,
         down_send,
         down_recv,
+        pass_send,
         low_send,
         low_recv,
         all_send,
@@ -51,6 +58,7 @@
         swap_recv,
     ) = rest[2 * stages :]
     me = lax.axis_index("wide")
+    group = lax.axis_index("groups")
     core = lax.rem(me, 2)
     chip = me // 2
     sibling = me + 1 - 2 * core
@@ -72,7 +80,14 @@
         return carry
 
     lax.fori_loop(1, devices, greet, 0)
-    pl.semaphore_wait(barrier, devices - 1)
+    for q in range(1, groups):
+        pl.semaphore_signal(
+            barrier,
+            inc=1,
+            device_id={"groups": lax.rem(group + q, groups), "wide": me},
+            device_id_type=pl.DeviceIdType.MESH,
+        )
+    pl.semaphore_wait(barrier, devices + groups - 2)
 
     def remote(src, dst, send, recv, to):
         return pltpu.make_async_remote_copy(
@@ -93,6 +108,17 @@
             to,
         )
 
+    def pass_copy(owner, q):
+        piece = down_all.at[pl.ds(pl.multiple_of(owner * rank, rank), rank)]
+        return pltpu.make_async_remote_copy(
+            src_ref=piece,
+            dst_ref=piece,
+            send_sem=pass_send.at[owner * groups + q],
+            recv_sem=down_recv.at[owner],
+            device_id={"groups": lax.rem(group + q, groups), "wide": me},
+            device_id_type=pl.DeviceIdType.MESH,
+        )
+
     def low_copy(to, owner):
         return remote(
             low_part.at[to], low_got.at[owner], low_send.at[to], low_recv.at[owner], to
@@ -126,12 +152,32 @@
 
         lax.fori_loop(1, devices, one, 0)
 
-    def each_chunk(action):
+    def each_chunk(action, first=0, end=None):
         def one(k, carry):
             action(k)
             return carry
 
-        lax.fori_loop(0, chunks, one, 0)
+        lax.fori_loop(first, chunks if end is None else end, one, 0)
+
+    bits = [lax.rem(chip // 2**s, 2) for s in range(stages)]
+    partners = [me + 2 ** (s + 1) * (1 - 2 * bits[s]) for s in range(stages)]
+
+    def half_copy(s, k):
+        return remote(
+            sends[s].at[k],
+            gots[s].at[k],
+            half_send.at[s * chunks + k],
+            half_recv.at[s * chunks + k],
+            partners[s],
+        )
+
+    half = rows // 2
+    away = pl.multiple_of((1 - bits[0]) * half, half)
+    kept = pl.multiple_of(bits[0] * half, half)
+    early_columns = EARLY * width
+
+    def fetched(peer):
+        return lax.rem(me + peer, groups) == group
 
     own_rank = pl.ds(pl.multiple_of(core * rank, rank), rank)
     acts_copy = remote(acts_ref, acts_sib, acts_sem.at[0], acts_sem.at[1], sibling)
@@ -152,7 +198,7 @@
         down_all.at[pl.ds(pl.multiple_of(me * rank, rank), rank)],
         down_send.at[me],
     )
-    each_peer(lambda peer: down_copy(peer, me).start())
+    each_peer(lambda peer: pl.when(fetched(peer))(lambda: down_copy(peer, me).start()))
     down_fetch.start()
     acts_copy.start()
 
@@ -173,24 +219,54 @@
             acts_ref[...], weight_own[k], preferred_element_type=jnp.float32
         ) + jnp.dot(acts_sib[...], weight_sib[k], preferred_element_type=jnp.float32)
 
-    each_chunk(base)
+    def base_early(k):
+        base(k)
+        sends[0][k] = total[k, pl.ds(away, half)].astype(jnp.bfloat16)
+        half_copy(0, k).start()
+
+    far_copy = remote(
+        up_pair.at[:, pl.ds(0, early_columns)], up_far, far_sem.at[0], far_sem.at[1], partners[0]
+    )
+    each_chunk(base_early, 0, EARLY)
+    up_fetch.wait()
+    up_copy.wait_recv()
+    far_copy.start()
+    each_chunk(base, EARLY)
 
     down_fetch.wait()
-    each_peer(lambda peer: down_copy(me, peer).wait_recv())
+
+    def arrive(peer):
+        @pl.when(fetched(peer))
+        def _():
+            down_copy(me, peer).wait_recv()
+            for q in range(1, groups):
+                pass_copy(peer, q).start()
+
+    def passed(peer):
+        @pl.when(jnp.logical_not(fetched(peer)))
+        def _():
+            down_copy(me, peer).wait_recv()
+
+    each_peer(arrive)
+    each_peer(passed)
     odd = (lax.broadcasted_iota(jnp.int32, (rows, 2 * rank), 1) >= rank).astype(jnp.int32)
     number = ids_ref[...] - odd
-    low_part[...] = jnp.zeros_like(low_part)
+    low_sum[...] = jnp.zeros_like(low_sum)
 
     def shrink(j, carry):
         pair = down_all[pl.ds(pl.multiple_of(j * 2 * rank, 2 * rank), 2 * rank)]
         part = lax.dot_general(
             acts_ref[...], pair, (((1,), (1,)), ((), ())), preferred_element_type=jnp.float32
         )
-        part = jnp.where(number == 2 * j, part, 0.0)
-        low_part[...] += part.reshape(devices, block, 2 * rank)
+        low_sum[...] += jnp.where(number == 2 * j, part, 0.0)
         return carry
 
     lax.fori_loop(0, devices // 2, shrink, 0)
+    pairs = rows // 2
+    left = lax.broadcasted_iota(jnp.int32, (devices, block // 2, 2 * rank), 2) < rank
+    both = low_sum[...] + pltpu.roll(low_sum[...], rank, 1)
+    both = both.reshape(devices, 2, block // 2, 2 * rank)
+    low_part[...] = jnp.where(left, both[:, 0], both[:, 1])
     each_peer(lambda peer: low_copy(peer, me).start())
 
     def gather(i, value):
@@ -201,24 +277,14 @@
     low_all[me] = lax.fori_loop(1, devices, gather, low_part[me]).astype(jnp.bfloat16)
     each_peer(lambda peer: all_copy(peer, me).start())
     each_peer(lambda peer: all_copy(me, peer).wait_recv())
-    everything = low_all[...].astype(jnp.float32).reshape(rows, 2 * rank)
+    packed = low_all[...].astype(jnp.float32)
+    turned = pltpu.roll(packed.reshape(pairs, 2 * rank), rank, 1).reshape(packed.shape)
+    upper, lower = jnp.where(left, packed, turned), jnp.where(left, turned, packed)
+    everything = jnp.stack([upper, lower], axis=1).reshape(rows, 2 * rank)
     low_mine[...] = jnp.where(number == 2 * chip, everything, 0.0).astype(jnp.bfloat16)
-    up_fetch.wait()
-    up_copy.wait_recv()
-
-    bits = [lax.rem(chip // 2**s, 2) for s in range(stages)]
-    partners = [me + 2 ** (s + 1) * (1 - 2 * bits[s]) for s in range(stages)]
-
-    def half_copy(s, k):
-        return remote(
-            sends[s].at[k],
-            gots[s].at[k],
-            half_send.at[s * chunks + k],
-            half_recv.at[s * chunks + k],
-            partners[s],
-        )
-
-    half = rows // 2
+    low_far[...] = jnp.where(number == 2 * (partners[0] // 2), everything, 0.0).astype(
+        jnp.bfloat16
+    )
 
     def delta(k, start):
         return jnp.dot(
@@ -227,9 +293,6 @@
             preferred_element_type=jnp.float32,
         )
 
-    away = pl.multiple_of((1 - bits[0]) * half, half)
-    kept = pl.multiple_of(bits[0] * half, half)
-
     def first(k):
         sends[0][k] = (total[k, pl.ds(away, half)] + delta(k, away)).astype(jnp.bfloat16)
         half_copy(0, k).start()
@@ -237,8 +300,15 @@
     def second(k):
         total[k, pl.ds(kept, half)] += delta(k, kept)
 
-    each_chunk(first)
-    each_chunk(second)
+    def second_far(k):
+        total[k, pl.ds(kept, half)] += jnp.dot(
+            low_far[pl.ds(kept, half)],
+            up_far[:, pl.ds(pl.multiple_of(k * width, width), width)],
+            preferred_element_type=jnp.float32,
+        )
+
+    each_chunk(first, EARLY)
+    far_copy.wait_recv()
 
     def swap_copy(k):
         return remote(
@@ -278,6 +348,8 @@
         offsets.append(offsets[-1] + bits[s] * sizes[-1])
 
     def step(t, carry):
+        pl.when(t < chunks)(lambda: second(t))
+        pl.when(t < EARLY)(lambda: second_far(t))
         for s in range(stages):
 
             @pl.when((t >= s) & (t - s < chunks))
@@ -306,16 +378,22 @@
     each_chunk(close)
 
     def close_peer(peer):
-        down_copy(peer, me).wait_send()
+        @pl.when(fetched(peer))
+        def _():
+            down_copy(peer, me).wait_send()
+            for q in range(1, groups):
+                pass_copy(peer, q).wait_send()
+
         low_copy(peer, me).wait_send()
         all_copy(peer, me).wait_send()
 
     each_peer(close_peer)
     acts_copy.wait_send()
     up_copy.wait_send()
-
-
-def shards(devices, acts, weight, down, up, numbers):
+    far_copy.wait_send()
+
+
+def shards(devices, groups, acts, weight, down, up, numbers):
     steps, rows, feats = acts.shape
     rank, columns = up.shape[1:]
     chips = devices // 2
@@ -331,11 +409,11 @@
 
     down = down.reshape(devices, feats, rank).swapaxes(1, 2)
     bf16, f32 = jnp.bfloat16, jnp.float32
-    low_block = (devices, total_rows // devices, 2 * rank)
+    low_block = (devices, total_rows // devices // 2, 2 * rank)
     halves = [(CHUNKS, total_rows >> (s + 1), width) for s in range(stages)]
     dma = pltpu.SemaphoreType.DMA
     out = pl.pallas_call(
-        functools.partial(kernel, devices, stages),
+        functools.partial(kernel, devices, groups, stages),
         out_shape=jax.ShapeDtypeStruct((2 * CHUNKS, steps * block, width), bf16),
         in_specs=[
             pl.BlockSpec(memory_space=pltpu.VMEM),
@@ -351,18 +429,23 @@
             pltpu.VMEM((CHUNKS, feats, width), bf16),
             pltpu.VMEM((devices * rank, feats), bf16),
             pltpu.VMEM((2 * rank, columns // 2), bf16),
+            pltpu.VMEM((2 * rank, EARLY * width), bf16),
             pltpu.VMEM((CHUNKS, total_rows, width), f32),
+            pltpu.VMEM((total_rows, 2 * rank), f32),
             pltpu.VMEM(low_block, f32),
             pltpu.VMEM(low_block, f32),
             pltpu.VMEM(low_block, bf16),
+            pltpu.VMEM((total_rows, 2 * rank), bf16),
             pltpu.VMEM((total_rows, 2 * rank), bf16),
             pltpu.VMEM((CHUNKS, steps * block, width), bf16),
         ]
         + [pltpu.VMEM(shape, bf16) for shape in halves]
         + [pltpu.VMEM(shape, bf16) for shape in halves]
-        + [dma((2,)), dma((3,))]
+        + [dma((2,)), dma((3,)), dma((2,))]
         + [dma((CHUNKS,))] * 3
-        + [dma((devices,))] * 6
+        + [dma((devices,))] * 2
+        + [dma((devices * groups,))]
+        + [dma((devices,))] * 4
         + [dma((stages * CHUNKS,))] * 2
         + [dma((CHUNKS,))] * 2,
         compiler_params=pltpu.CompilerParams(
@@ -383,7 +466,7 @@
     )
     out_specs = P(None, ("groups", "wide"), None)
     return jax.shard_map(
-        functools.partial(shards, mesh.shape["wide"]),
+        functools.partial(shards, mesh.shape["wide"], mesh.shape["groups"]),
         mesh=mesh,
         in_specs=in_specs,
         out_specs=out_specs,

time: 117 us -> 98.3 us (0.84)
  Pallas kernels: 108 us -> 89.3 us
    pallas_call x1, Pallas kernels: 108 us -> 89.3 us  [shards(): pl.pallas_call(functools.partial(kernel, devices, groups, stages), out_sh...]
where the time goes in v2:
time: 98.3 us; the launch traced here: 97.9 us
  Pallas kernels  89.3 us (91%)
  local copies, waits for them, and re-layouts  7.88 us (8%)
    pallas_call x1, Pallas kernels, shards(): pl.pallas_call(functools.partial(kernel, devices, groups, stages), out_sh...  89.3 us
    reshape x3, local copies, waits for them, and re-layouts, arranged(): array.reshape((steps,) + (2,) * stages + (2, block, array.shape[-1]))  1.98 us

profile of v2, /device:TPU:0, one launch (start us, length us, event | category | flops | bytes accessed | tf_op | source)
XLA Modules:
  0.0 97.9 jit_solution(3249130208065237129)
XLA Ops:
  0.0 1.6 %copy.15 = bf16[8,8,16,512]{3,2,1,0:T(8,128)(2,1)S(1)} copy(bf16[8,8,16,512]{3,1,2,0:T(8,128)(2,1)} %bitcast.28) | data formatting | bytes 2097152
  1.6 1.6 %copy.18 = bf16[16,512,64]{1,2,0:T(8,128)(2,1)} copy(bf16[16,512,64]{1,0,2:T(8,128)(2,1)S(1)} %bitcast.24) | data formatting | bytes 2097152 | tf_op jit(solution)/shard_map/reshape | solution.py:410
  3.1 1.9 %copy.10 = bf16[2,2,2,2,2,16,512]{6,5,0,4,1,2,3:T(8,128)(2,1)} copy(bf16[2,2,2,2,2,16,512]{6,5,4,3,2,1,0:T(8,128)(2,1)} %bitcast.29) | data formatting | bytes 1048576 | tf_op jit(solution)/shard_map/reshape | solution.py:407
  5.0 0.7 reduce
  5.7 0.1 reshape.24
  5.8 0.9 reshape.32.ids_ref
  6.7 89.3 %shard_map.55 = bf16[16,32,512]{2,1,0:T(8,128)(2,1)} custom-call(s32[512,1]{1,0:T(8,128)} %reshape.32.ids_ref, bf16[512,512]{1,0:T(8,128)(2,1)} %bitcast.25, bf16[512,8192]{1,0:T(8,128)(2,1)} %weight_ref.1, bf16[16,64,512]{2,1,0:T(8,128)(2,1)} %bitcast.23, bf16[64,8192]{1,0:T(8,128)(2,1)} %bitcast.27), custom_call_target="tpu_custom_call" | custom-call | tf_op jit(solution)/shard_map/pallas_call | solution.py:415
  96.0 1.9 %copy.14 = bf16[16,2,2,8,512]{4,3,0,2,1:T(8,128)(2,1)} copy(bf16[16,2,2,8,512]{4,3,2,1,0:T(8,128)(2,1)} %bitcast.26) | data formatting | bytes 1048576 | tf_op jit(solution)/shard_map/reshape | solution.py:456
  (1 shorter events, 0.0 us)

commit v3 on v2

--- a/solution.py
+++ b/solution.py
@@ -16,11 +16,12 @@
     groups,
     stages,
     ids_ref,
-    acts_ref,
+    acts_given,
     weight_ref,
     down_ref,
     up_ref,
     out_ref,
+    acts_ref,
     acts_sib,
     weight_own,
     weight_sib,
@@ -39,6 +40,7 @@
 ):
     sends, gots = rest[:stages], rest[stages : 2 * stages]
     (
+        acts_local,
         acts_sem,
         up_sem,
         far_sem,
@@ -68,6 +70,30 @@
     half_columns = chunks * width
     block = rows // devices
 
+    steps = acts_given.shape[0]
+    share = block // steps
+
+    def acts_fetch(i):
+        host, step = i // steps, lax.rem(i, steps)
+        place = lax.rem(host, 2)
+        for s in range(stages):
+            place += lax.rem(host // 2 ** (s + 1), 2) * 2 ** (stages - s)
+        return pltpu.make_async_copy(
+            acts_given.at[step, pl.ds(pl.multiple_of(host * share, share), share)],
+            acts_ref.at[pl.ds(pl.multiple_of((place * steps + step) * share, share), share)],
+            acts_local.at[i],
+        )
+
+    def fetch(i, carry):
+        acts_fetch(i).start()
+        return carry
+
+    def fetch_end(i, carry):
+        acts_fetch(i).wait()
+        return carry
+
+    lax.fori_loop(0, devices * steps, fetch, 0)
+
     barrier = pltpu.get_barrier_semaphore()
 
     def greet(i, carry):
@@ -200,6 +226,7 @@
     )
     each_peer(lambda peer: pl.when(fetched(peer))(lambda: down_copy(peer, me).start()))
     down_fetch.start()
+    lax.fori_loop(0, devices * steps, fetch_end, 0)
     acts_copy.start()
 
     def load(k):
@@ -417,13 +444,14 @@
         out_shape=jax.ShapeDtypeStruct((2 * CHUNKS, steps * block, width), bf16),
         in_specs=[
             pl.BlockSpec(memory_space=pltpu.VMEM),
-            pl.BlockSpec(memory_space=pltpu.VMEM),
+            pl.BlockSpec(memory_space=pl.ANY),
             pl.BlockSpec(memory_space=pl.ANY),
             pl.BlockSpec(memory_space=pl.ANY),
             pl.BlockSpec(memory_space=pl.ANY),
         ],
         out_specs=pl.BlockSpec(memory_space=pltpu.VMEM),
         scratch_shapes=[
+            pltpu.VMEM((total_rows, feats), bf16),
             pltpu.VMEM((total_rows, feats), bf16),
             pltpu.VMEM((CHUNKS, feats, width), bf16),
             pltpu.VMEM((CHUNKS, feats, width), bf16),
@@ -441,7 +469,7 @@
         ]
         + [pltpu.VMEM(shape, bf16) for shape in halves]
         + [pltpu.VMEM(shape, bf16) for shape in halves]
-        + [dma((2,)), dma((3,)), dma((2,))]
+        + [dma((steps * devices,)), dma((2,)), dma((3,)), dma((2,))]
         + [dma((CHUNKS,))] * 3
         + [dma((devices,))] * 2
         + [dma((devices * groups,))]
@@ -451,7 +479,7 @@
         compiler_params=pltpu.CompilerParams(
             collective_id=0, has_side_effects=True, vmem_limit_bytes=58 * 1024 * 1024
         ),
-    )(arranged(numbers), arranged(acts), weight, down, up.reshape(rank, columns))
+    )(arranged(numbers), acts, weight, down, up.reshape(rank, columns))
     out = out.reshape(2 * CHUNKS, steps, block, width).transpose(1, 2, 0, 3)
     return out.reshape(steps, block, columns)
 

time: 98.3 us -> 97 us (0.987)
  local copies, waits for them, and re-layouts: 7.88 us -> 6 us
    reshape x3 -> x2, local copies, waits for them, and re-layouts: 1.98 us -> 0.1 us  [arranged(): array.reshape((steps,) + (2,) * stages + (2, block, array.shape[-1]))]
where the time goes in v3:
time: 97 us; the launch traced here: 96.8 us
  Pallas kernels  90 us (93%)
  local copies, waits for them, and re-layouts  6 us (6%)
    pallas_call x1, Pallas kernels, shards(): pl.pallas_call(functools.partial(kernel, devices, groups, stages), out_sh...  90 us

profile of v3, /device:TPU:0, one launch (start us, length us, event | category | flops | bytes accessed | tf_op | source)
XLA Modules:
  0.0 96.8 jit_solution(10669247727787594999)
XLA Ops:
  0.0 1.6 %copy.13 = bf16[8,8,16,512]{3,2,1,0:T(8,128)(2,1)S(1)} copy(bf16[8,8,16,512]{3,1,2,0:T(8,128)(2,1)} %bitcast.23) | data formatting | bytes 2097152
  1.6 1.6 %copy.16 = bf16[16,512,64]{1,2,0:T(8,128)(2,1)} copy(bf16[16,512,64]{1,0,2:T(8,128)(2,1)S(1)} %bitcast.20) | data formatting | bytes 2097152 | tf_op jit(solution)/shard_map/reshape | solution.py:437
  3.1 0.7 reduce
  3.8 0.1 reshape.18
  4.0 0.9 reshape.24.ids_ref
  4.8 90.0 %shard_map.55 = bf16[16,32,512]{2,1,0:T(8,128)(2,1)} custom-call(s32[512,1]{1,0:T(8,128)} %reshape.24.ids_ref, bf16[2,256,512]{2,1,0:T(8,128)(2,1)} %acts_given.1, bf16[512,8192]{1,0:T(8,128)(2,1)} %weight_ref.1, bf16[16,64,512]{2,1,0:T(8,128)(2,1)} %bitcast.19, bf16[64,8192]{1,0:T(8,128)(2,1)} %bitcast.22), custom_call_target="tpu_custom_call" | custom-call | tf_op jit(solution)/shard_map/pallas_call | solution.py:442
  94.9 1.9 %copy.12 = bf16[16,2,2,8,512]{4,3,0,2,1:T(8,128)(2,1)} copy(bf16[16,2,2,8,512]{4,3,2,1,0:T(8,128)(2,1)} %bitcast.21) | data formatting | bytes 1048576 | tf_op jit(solution)/shard_map/reshape | solution.py:484
  (1 shorter events, 0.0 us)
